TPU v7x, 256 devices: a whole 4x4x8 slice. The times are simulated.
256 devices in a mesh: gx: 16 (over y_lo, z), gz: 8 (over x, y_hi), gy: 2 (over core).
Axes of the slice: x: 4, y: 4 (y_hi: 2, y_lo: 2; y = y_hi * 2 + y_lo), z: 8, core: 2. Of those that a mesh axis runs over, the one named last changes fastest.
Arguments:
- field: bfloat16 [8, 384, 384, 256], P(None, 'gx', 'gz', 'gy'), may hold values from -25 to 25
- x_factor: bfloat16 [384, 48], P('gx'), may hold values from -0.3125 to 0.3125
- y_factor: bfloat16 [256, 48], P('gy'), may hold values from -0.375 to 0.375
- species_basis_matrix: float32 [8, 4], replicated, may hold values from -2 to 2
Outputs:
- gram: float32 [384, 384], P('gz')
All inputs are finite; a program needn't handle non-finite values.
Results may differ from a plain program's by a relative error of at most 0.0003.
Values may be sent and summed in bfloat16 or wider, within the bound.
A program may use at most 64 MiB of HBM per device.

v0:
```python
import jax
import jax.numpy as jnp
from jax import lax
from jax.sharding import PartitionSpec as P


def x_terms(source, x_float, planes, count):
    result = jnp.einsum("xi,nxz->niz", x_float, source, precision=lax.Precision.HIGHEST)
    return result.reshape(count, planes)


def body(field, x_factor, y_factor, species_basis_matrix):
    species_count = field.shape[0]
    breadth = field.shape[1]
    planes = field.shape[2]
    first_rank = x_factor.shape[1]
    second_rank = y_factor.shape[1]
    species_target_rank = species_basis_matrix.shape[1]
    flat = field.reshape(species_count * breadth * planes, field.shape[3])
    across_y_axis = lax.dot_general(
        y_factor, flat, (((0,), (1,)), ((), ())), preferred_element_type=jnp.float32
    )
    across_y_axis = across_y_axis.reshape(second_rank, species_count, breadth * planes)
    reduced_tensor = jnp.einsum(
        "qtb,tf->qfb", across_y_axis, species_basis_matrix, precision=lax.Precision.HIGHEST
    )
    reduced_tensor = reduced_tensor.reshape(second_rank * species_target_rank, breadth, planes)
    x_float = x_factor.astype(jnp.float32)
    share = reduced_tensor.shape[0] // (lax.axis_size("gx") * lax.axis_size("gy")) * first_rank
    core = lax.psum_scatter(
        x_terms(reduced_tensor, x_float, planes, share * lax.axis_size(("gx", "gy"))),
        ("gx", "gy"),
        scatter_dimension=0,
        tiled=True,
    )
    blocks = lax.dot_general(
        core,
        lax.all_gather(core, "gz", axis=1, tiled=True),
        (((0,), (0,)), ((), ())),
        precision=lax.Precision.HIGHEST,
        preferred_element_type=jnp.float32,
    )
    summed_tensor = lax.psum(blocks, ("gx", "gy"))
    return summed_tensor / (first_rank * second_rank * species_target_rank)


def solution(mesh):
    placed = (P(None, "gx", "gz", "gy"), P("gx", None), P("gy", None), P())
    return jax.shard_map(body, mesh=mesh, in_specs=placed, out_specs=P("gz", None), check_vma=False)
```

profile of v0, /device:TPU:1, one launch (start us, length us, event | category | flops | bytes accessed | tf_op | source)
XLA Modules:
  0.0 384.7 jit_solution(4617105996399417866)
XLA Ops:
  6.5 0.0 copy-start
  6.5 0.0 reduce-scatter.4.cloned.1.call-start
  6.5 1.7 copy-done
  8.2 0.0 copy-start.2
  8.2 1.6 fusion.1
  9.8 0.0 copy-done.2
  9.9 2.0 convolution_bitcast_fusion
  11.9 2.7 reshape.10
  14.6 0.0 copy-start.1
  14.6 2.4 copy.9
  17.0 0.0 copy-done.1
  17.0 2.6 convolution_bitcast_fusion.1
  19.6 5.8 %copy.13 = f32[192,48,48]{2,1,0:T(8,128)} copy(f32[192,48,48]{0,1,2:T(8,128)} %convolution_bitcast_fusion.1) | data formatting | bytes 3538944
  25.3 0.0 reduce-scatter.4.cloned.1.call-update
  25.4 0.0 all-reduce.2.cloned.1.call-start
  25.4 123.0 %reduce-scatter.4.cloned.1.call-done = f32[288,48]{1,0:T(8,128)} async-done(((f32[9216,48]{1,0:T(8,128)}), f32[288,48]{1,0:T(8,128)}) %reduce-scatter.4.cloned.1.call-update) | async-done | bytes 55312
  148.4 1.0 copy.12
  149.4 29.6 %all_gather.3 = f32[288,384]{0,1:T(8,128)S(1)} all-gather(f32[288,48]{0,1:T(8,128)S(1)} %copy.12), channel_id=1, replica_groups=mesh['gx'=16,'gz'=8,'gy'=2] {'gz'}, dimensions={1}, use_global_device_ids=true | all-gather | bytes 497664 | tf_op jit(solution)/shard_map/all_gather | solution.py:38
  179.1 2.3 fusion.5
  181.4 0.0 all-reduce.2.cloned.1.call-update
  181.4 195.0 %all-reduce.2.cloned.1.call-done = f32[48,384]{1,0:T(8,128)} async-done(((f32[48,384]{1,0:T(8,128)}), f32[48,384]{1,0:T(8,128)}) %all-reduce.2.cloned.1.call-update) | async-done | bytes 73744 | tf_op jit(solution)/shard_map/psum | solution.py:43
  376.4 1.5 broadcast_multiply_fusion
Async XLA Ops:
  6.5 1.7 copy-start
  6.5 141.9 %reduce-scatter.4.cloned.1.call-start = ((), (), s32[]{:S(2)}) async-start(), calls=%async_computation.2 | async-start | bytes 4866048
  8.2 1.7 copy-start.2
  14.6 2.4 copy-start.1
  25.4 351.0 %all-reduce.2.cloned.1.call-start = ((), (), s32[]{:S(2)}) async-start(), calls=%async_computation.1 | async-start | bytes 147456 | tf_op jit(solution)/shard_map/psum | solution.py:43
Sparse Core Ops, SparseCore 0:
  25.5 122.9 reduce-scatter.3
  181.5 194.7 all-reduce.1
where the time goes:
time: 386 us; the launch traced here: 385 us
  waiting for transfers between devices  318 us (82%)
  blocking collectives  29.6 us (8%)
  local copies, waits for them, and re-layouts  13.5 us (3%)
  between operations  13.4 us (3%)
  matrix products  8.57 us (2%)
    psum x1, waiting for transfers between devices, body(): summed_tensor = lax.psum(blocks, ('gx', 'gy'))  195 us
    unnamed x3, waiting for transfers between devices  123 us
    all_gather x1, blocking collectives, body(): lax.all_gather(core, 'gz', axis=1, tiled=True)  29.6 us
    unnamed x8, local copies, waits for them, and re-layouts  8.47 us
  transfers between devices with their start and end apart: 2, of which 2 were waited for; matrix products, arithmetic and copies ran while one was open for 0% of the time, Pallas kernels for 0%

commit v1 on v0

v1 whole, which is shorter than its diff:
```python
import functools

import jax
import jax.numpy as jnp
from jax import lax
from jax.experimental import pallas as pl
from jax.experimental.pallas import tpu as pltpu
from jax.sharding import PartitionSpec as P

MESH = pl.DeviceIdType.MESH
F32 = jnp.float32
BF16 = jnp.bfloat16
NT = (((1,), (1,)), ((), ()))

NGX, NGZ, NGY = 16, 8, 2
XL, ZL = 24, 48
RI, RJ, RP, NS = 48, 48, 4, 8
ZG, ZZ = 10, 5
TOP = 32000.0
BIAS = 124.0
SHARE = 6
CH = 4
ROWS = XL * ZL // CH


def encode(value, inverse):
    whole = jnp.round(value * inverse)
    size = jnp.abs(whole)
    high = jnp.floor(size * (1.0 / 128.0))
    code = jnp.exp2(high - BIAS) * (1.0 + (size - 128.0 * high) * (1.0 / 128.0))
    return jnp.where(whole < 0.0, -code, code)


def decode(code):
    size = jnp.abs(code)
    high = jnp.floor(jnp.log2(size) + 0.002)
    whole = jnp.round(128.0 * (high + (BIAS - 1.0) + size * jnp.exp2(-high)))
    return jnp.where(code < 0.0, -whole, whole)


def scale_of(largest):
    unit = (largest * (1.01 / TOP)).astype(BF16).astype(F32)
    return jnp.maximum(unit, 2.0**-100)


def split(value):
    high = value.astype(BF16)
    return high, (value - high.astype(F32)).astype(BF16)


def kernel(field, xf, yf, sb, out, fbuf, whi, wlo, mine, other, prt, tsum, xsend, xrecv, bd, asend, arecv, acc, d2,
           cbuf, chi, clo, gpart, rrecv, red, ofull,
           f_sem, es_sem, er_sem, xs_sem, xr_sem, as_sem, ar_sem, cs_sem, cr_sem, rs_sem, rr_sem, bs_sem, br_sem):
    gx, gz, gy = lax.axis_index("gx"), lax.axis_index("gz"), lax.axis_index("gy")
    line = gx * 2 + gy

    def to_gx(dd):
        return {"gx": (gx + dd) % NGX, "gz": gz, "gy": gy}

    def to_gz(e):
        return {"gx": gx, "gz": (gz + e) % NGZ, "gy": gy}

    def to_line(k):
        there = (line + k) % 32
        return {"gx": there // 2, "gz": gz, "gy": there % 2}

    loads = []
    for c in range(CH):
        part = pl.ds(c * (XL // CH), XL // CH)
        loads.append(pltpu.make_async_copy(field.at[:, part], fbuf.at[:, part], f_sem.at[c]))
        loads[-1].start()

    barrier = pltpu.get_barrier_semaphore()

    def greet(k, _):
        pl.semaphore_signal(barrier, inc=1, device_id=to_line(k), device_id_type=MESH)
        return 0

    lax.fori_loop(1, 32, greet, 0)
    for e in range(1, NGZ):
        pl.semaphore_signal(barrier, inc=1, device_id=to_gz(e), device_id_type=MESH)

    x32 = xf[...].astype(F32)
    low = jnp.concatenate([x32[16:24], jnp.zeros((8, RI), F32)], axis=0)
    gap = jnp.zeros((16, 16), F32)
    xsend[...] = jnp.concatenate([x32[0:16], gap, low, gap], axis=1).astype(BF16)

    lane = lax.broadcasted_iota(jnp.int32, (RJ, 256), 1)
    q = lane & 7
    dest = (gx + ((lane >> 3) & 15)) & 15
    late = (q >= 3).astype(jnp.int32)
    jl = 3 * dest + q - 3 * late
    pick = (lax.broadcasted_iota(jnp.int32, (RJ, 256), 0) == jl) & (q < SHARE)
    spread = jnp.dot(yf[...], pick.astype(F32).astype(BF16), preferred_element_type=F32)
    plane = (2 * (((lane >> 7) + gy) & 1) + late)[0:NS]
    basis = sb[...]
    mix = jnp.zeros((NS, 256), F32)
    for p in range(RP):
        mix = mix + jnp.where(plane == p, basis[:, p:p + 1], 0.0)
    for s in range(NS):
        high, rest = split(spread * mix[s:s + 1, :])
        whi[128 * s:128 * s + 128, :] = high
        wlo[128 * s:128 * s + 128, :] = rest

    pl.semaphore_wait(barrier, 31 + NGZ - 1)

    xcopies = [
        pltpu.make_async_remote_copy(xsend, xrecv.at[dd], xs_sem.at[dd], xr_sem.at[dd], device_id=to_gx(dd), device_id_type=MESH)
        for dd in range(1, NGX)
    ]
    for copy in xcopies:
        copy.start()

    exchanges = []
    for c in range(CH):
        loads[c].wait()
        left = jnp.concatenate(
            [fbuf[s, c * (XL // CH):(c + 1) * (XL // CH)].reshape(ROWS, 128) for s in range(NS)], axis=1)
        part = jnp.dot(left, whi[...], preferred_element_type=F32) + jnp.dot(left, wlo[...], preferred_element_type=F32)
        span = pl.ds(c * ROWS, ROWS)
        mine[span, :] = part[:, 0:128]
        other[span, :] = part[:, 128:256]
        exchanges.append(pltpu.make_async_remote_copy(
            other.at[span], prt.at[span], es_sem.at[c], er_sem.at[c],
            device_id={"gx": gx, "gz": gz, "gy": 1 - gy}, device_id_type=MESH))
        exchanges[-1].start()

    largest = jnp.zeros((8, 128), F32)
    for c in range(CH):
        exchanges[c].wait_recv()
        span = pl.ds(c * ROWS, ROWS)
        total = mine[span, :] + prt[span, :]
        tsum[span, :] = total
        largest = jnp.maximum(largest, jnp.max(jnp.abs(total).reshape(ROWS // 8, 8, 128), axis=0))
    unit = scale_of(jnp.max(largest, keepdims=True))
    inverse = 1.0 / unit

    is_scale = lax.broadcasted_iota(jnp.int32, (NGX, 8, 128), 1) == SHARE

    def coded(zg):
        pieces = []
        for zz in range(ZZ):
            z = zg + ZG * zz
            pieces.append(tsum[pl.ds(z, XL, stride=ZL), :] if z < ZL else jnp.zeros((XL, 128), F32))
        pieces.append(jnp.zeros((8, 128), F32))
        tile = jnp.concatenate(pieces, axis=0).T
        return jnp.where(is_scale, unit.reshape(1, 1, 1), encode(tile, inverse).reshape(NGX, 8, 128))

    for m in range(ZG // 2):
        both = jnp.concatenate([coded(2 * m), coded(2 * m + 1)], axis=1)
        asend[:, 16 * m:16 * m + 16, :] = both.astype(BF16)

    acopies = {
        dd: pltpu.make_async_remote_copy(asend.at[dd], arecv.at[dd], as_sem.at[dd], ar_sem.at[dd], device_id=to_gx(dd), device_id_type=MESH)
        for dd in range(1, NGX)
    }
    for dd in range(1, NGX):
        acopies[dd].start()

    for copy in xcopies:
        copy.wait_recv()
    xrecv[0] = xsend[...]
    row = lax.broadcasted_iota(jnp.int32, (128, 256), 0)
    lane = lax.broadcasted_iota(jnp.int32, (128, 256), 1)
    slot = jnp.zeros((128, 256), jnp.int32)
    for zz in range(1, ZZ):
        slot = slot + (lane >= RI * zz).astype(jnp.int32)
    want = lane - RI * slot
    first = ((row == want) & (lane < RI * ZZ)).astype(F32).astype(BF16)
    second = ((row == want + 64) & (lane < RI * ZZ)).astype(F32).astype(BF16)
    everything = xrecv[...].reshape(NGX * 16, 128)
    upper = jnp.dot(everything, first, preferred_element_type=F32)
    lower = jnp.dot(everything, second, preferred_element_type=F32)
    column = slot[0:XL]
    for dd in range(NGX):
        block = jnp.concatenate([upper[16 * dd:16 * dd + 16], lower[16 * dd:16 * dd + 8]], axis=0)
        stack = [jnp.where(column == zz, block, 0.0) for zz in range(ZZ)] + [jnp.zeros((8, 256), F32)]
        bd[128 * dd:128 * dd + 128, :] = jnp.concatenate(stack, axis=0).astype(BF16)

    for k in range(NGX // 2):
        sides = []
        for dd in (2 * k, 2 * k + 1):
            if dd:
                acopies[dd].wait_recv()
            held = (arecv if dd else asend)[dd].astype(F32)
            sides.append(decode(held) * held[SHARE:SHARE + 1, :])
        high, rest = split(jnp.concatenate(sides, axis=1))
        product = jnp.dot(jnp.concatenate([high, rest], axis=0), bd[256 * k:256 * k + 256, :], preferred_element_type=F32)
        if k == 0:
            acc[...] = product
        else:
            acc[...] += product

    core = acc[0:80, :] + acc[80:160, :]
    for zz in range(ZZ):
        d2[80 * zz:80 * zz + 80, 0:RI] = core[:, RI * zz:RI * zz + RI]
    rows = jnp.concatenate([d2[pl.ds(c, ZL, stride=8), :][:, 0:RI] for c in range(SHARE)], axis=1)
    unit = scale_of(jnp.max(jnp.abs(rows), keepdims=True))
    words = jnp.concatenate([encode(rows, 1.0 / unit), jnp.broadcast_to(unit, (ZL, 96))], axis=1)
    cbuf[gz] = words.astype(BF16)

    ccopies = [
        pltpu.make_async_remote_copy(cbuf.at[gz], cbuf.at[gz], cs_sem.at[e], cr_sem.at[e], device_id=to_gz(e), device_id_type=MESH)
        for e in range(1, NGZ)
    ]
    for copy in ccopies:
        copy.start()
    for copy in ccopies:
        copy.wait_recv()

    real = lax.broadcasted_iota(jnp.int32, (ZL, 384), 1) < SHARE * RI
    for z0 in range(NGZ):
        held = cbuf[z0].astype(F32)
        high, rest = split(jnp.where(real, decode(held) * held[:, 288:289], 0.0))
        chi[ZL * z0:ZL * z0 + ZL, :] = high
        clo[ZL * z0:ZL * z0 + ZL, :] = rest
    own = pl.ds(pl.multiple_of(gz * ZL, 16), ZL)
    left = jnp.concatenate([chi[own, :], clo[own, :]], axis=0)
    gram = lax.dot_general(left, chi[...], NT, preferred_element_type=F32) + lax.dot_general(left, clo[...], NT, preferred_element_type=F32)
    gram = (gram[0:ZL] + gram[ZL:2 * ZL]) * (1.0 / (RI * RJ * RP))
    for a in range(6):
        for b in range(3):
            gpart[3 * a + b] = gram[8 * a:8 * a + 8, 128 * b:128 * b + 128]

    reducer = (gy == 0) | (gx % 8 == 0)
    tile = jnp.where(gy == 0, gx, 16 + gx // 8)

    def shipment(r):
        there = {"gx": r, "gz": gz, "gy": 0} if r < 16 else {"gx": 8 * (r - 16), "gz": gz, "gy": 1}
        return pltpu.make_async_remote_copy(gpart.at[r], rrecv.at[line], rs_sem.at[r], rr_sem, device_id=there, device_id_type=MESH)

    for r in range(18):
        @pl.when(jnp.logical_not(reducer & (tile == r)))
        def _():
            shipment(r).start()

    def spread_out(k):
        return pltpu.make_async_remote_copy(red, ofull.at[tile], bs_sem.at[k], br_sem.at[tile], device_id=to_line(k), device_id_type=MESH)

    @pl.when(reducer)
    def _():
        rrecv[line] = gpart[tile]
        rest = rrecv.at[pl.ds(0, 31)]
        pltpu.make_async_copy(rest, rest, rr_sem).wait()
        summed = rrecv[0]
        for k in range(1, 32):
            summed = summed + rrecv[k]
        red[...] = summed
        ofull[tile] = summed

        def send(k, _):
            spread_out(k).start()
            return 0

        lax.fori_loop(1, 32, send, 0)

    for r in range(18):
        @pl.when(jnp.logical_not(reducer & (tile == r)))
        def _():
            pltpu.make_async_copy(ofull.at[r], ofull.at[r], br_sem.at[r]).wait()

    for a in range(6):
        for b in range(3):
            out[8 * a:8 * a + 8, 128 * b:128 * b + 128] = ofull[3 * a + b]

    for copy in xcopies + exchanges + list(acopies.values()) + ccopies:
        copy.wait_send()
    for r in range(18):
        @pl.when(jnp.logical_not(reducer & (tile == r)))
        def _():
            shipment(r).wait_send()

    @pl.when(reducer)
    def _():
        def finish(k, _):
            spread_out(k).wait_send()
            return 0

        lax.fori_loop(1, 32, finish, 0)


def body(field, x_factor, y_factor, species_basis_matrix):
    vmem = pl.BlockSpec(memory_space=pltpu.VMEM)
    dma = pltpu.SemaphoreType.DMA
    return pl.pallas_call(
        kernel,
        out_shape=jax.ShapeDtypeStruct((ZL, NGZ * ZL), F32),
        in_specs=[pl.BlockSpec(memory_space=pl.ANY), vmem, vmem, vmem],
        out_specs=vmem,
        scratch_shapes=[
            pltpu.VMEM((NS, XL, ZL, 128), BF16),
            pltpu.VMEM((1024, 256), BF16),
            pltpu.VMEM((1024, 256), BF16),
            pltpu.VMEM((XL * ZL, 128), F32),
            pltpu.VMEM((XL * ZL, 128), F32),
            pltpu.VMEM((XL * ZL, 128), F32),
            pltpu.VMEM((XL * ZL, 128), F32),
            pltpu.VMEM((16, 128), BF16),
            pltpu.VMEM((NGX, 16, 128), BF16),
            pltpu.VMEM((NGX * 128, 256), BF16),
            pltpu.VMEM((NGX, 80, 128), BF16),
            pltpu.VMEM((NGX, 80, 128), BF16),
            pltpu.VMEM((160, 256), F32),
            pltpu.VMEM((400, 128), F32),
            pltpu.VMEM((NGZ, ZL, 384), BF16),
            pltpu.VMEM((NGZ * ZL, 384), BF16),
            pltpu.VMEM((NGZ * ZL, 384), BF16),
            pltpu.VMEM((18, 8, 128), F32),
            pltpu.VMEM((32, 8, 128), F32),
            pltpu.VMEM((8, 128), F32),
            pltpu.VMEM((18, 8, 128), F32),
            dma((CH,)), dma((CH,)), dma((CH,)), dma((NGX,)), dma((NGX,)), dma((NGX,)), dma((NGX,)),
            dma((NGZ,)), dma((NGZ,)), dma((18,)), dma, dma((32,)), dma((18,)),
        ],
        compiler_params=pltpu.CompilerParams(collective_id=0, has_side_effects=True, vmem_limit_bytes=40 * 1024 * 1024),
    )(field, x_factor, y_factor, species_basis_matrix)


def solution(mesh):
    placed = (P(None, "gx", "gz", "gy"), P("gx", None), P("gy", None), P())
    return jax.shard_map(body, mesh=mesh, in_specs=placed, out_specs=P("gz", None), check_vma=False)
```

time: 386 us -> 51.1 us (0.13)
  waiting for transfers between devices: 318 us -> 0 us
  Pallas kernels: 0 us -> 46.3 us
  blocking collectives: 29.6 us -> 0 us
  between operations: 13.4 us -> 0.02 us
  local copies, waits for them, and re-layouts: 13.5 us -> 4.57 us
  matrix products: 8.57 us -> 0 us
    psum x1 -> x0, waiting for transfers between devices: 195 us -> none  [body(): summed_tensor = lax.psum(blocks, ('gx', 'gy'))]
    unnamed x3 -> x0, waiting for transfers between devices: 123 us -> none
    pallas_call x0 -> x1, Pallas kernels: none -> 46.3 us  [body(): pl.pallas_call(kernel, out_shape=jax.ShapeDtypeStruct((ZL, NGZ * ZL), F32...]
    all_gather x1 -> x0, blocking collectives: 29.6 us -> none  [body(): lax.all_gather(core, 'gz', axis=1, tiled=True)]
    dot_general x4 -> x0, matrix products: 8.57 us -> none  [the longest x1 2.57 us: x_terms(): jnp.einsum('xi,nxz->niz', x_float, source, precision=lax.Precision.HIGHEST)]
    reshape x2 -> x0, local copies, waits for them, and re-layouts: 5.06 us -> none  [body(): reduced_tensor.reshape(second_rank * species_target_rank, breadth, planes)]
    unnamed x8 -> x7, local copies, waits for them, and re-layouts: 8.47 us -> 4.57 us
  transfers between devices with their start and end apart: 2 -> 0, of which waited for: 2 -> 0; matrix products, arithmetic and copies ran while one was open for 0% -> 0% of each run, Pallas kernels for 0% -> 0%
where the time goes in v1:
time: 51.1 us; the launch traced here: 50.8 us
  Pallas kernels  46.3 us (91%)
  local copies, waits for them, and re-layouts  4.57 us (9%)
    pallas_call x1, Pallas kernels, body(): pl.pallas_call(kernel, out_shape=jax.ShapeDtypeStruct((ZL, NGZ * ZL), F32...  46.3 us
    unnamed x7, local copies, waits for them, and re-layouts  4.57 us

profile of v1, /device:TPU:1, one launch (start us, length us, event | category | flops | bytes accessed | tf_op | source)
XLA Modules:
  0.0 50.8 jit_solution(1964582996987091740)
XLA Ops:
  0.0 0.8 %copy.6.sb = f32[8,4]{1,0:T(8,128)S(1)} copy(f32[8,4]{0,1:T(4,128)} %param.7) | data formatting | bytes 256 | tf_op args[3]
  0.8 0.8 %copy.5.yf = bf16[128,48]{1,0:T(8,128)(2,1)S(1)} copy(bf16[128,48]{0,1:T(8,128)(2,1)} %param.6) | data formatting | bytes 24576 | tf_op args[2]
  1.6 0.0 copy-start
  1.6 1.7 %copy-done = bf16[8,24,48,128]{3,2,1,0:T(8,128)(2,1)S(1)} copy-done((bf16[8,24,48,128]{3,2,1,0:T(8,128)(2,1)S(1)}, bf16[8,24,48,128]{3,2,1,0:T(8,128)(2,1)}, u32[]{:S(2)}) %copy-start) | copy-done | bytes 2359320
  3.2 0.0 copy-start.1
  3.3 0.7 %copy-done.1 = bf16[24,48]{1,0:T(8,128)(2,1)S(1)} copy-done((bf16[24,48]{1,0:T(8,128)(2,1)S(1)}, bf16[24,48]{1,0:T(8,128)(2,1)}, u32[]{:S(2)}) %copy-start.1) | copy-done | bytes 2328
  3.9 46.3 %shard_map.46 = f32[48,384]{1,0:T(8,128)S(1)} custom-call(bf16[8,24,48,128]{3,2,1,0:T(8,128)(2,1)S(1)} %copy-done, bf16[24,48]{1,0:T(8,128)(2,1)S(1)} %copy-done.1, bf16[128,48]{1,0:T(8,128)(2,1)S(1)} %copy.5.yf, f32[8,4]{1,0:T(8,128)S(1)} %copy.6.sb), custom_call_target="tpu_custom_call" | custom-call | tf_op jit(solution)/shard_map/pallas_call | solution.py:285
  50.2 0.6 %copy.8 = f32[48,384]{1,0:T(8,128)} copy(f32[48,384]{1,0:T(8,128)S(1)} %shard_map.46) | data formatting | bytes 147456
Async XLA Ops:
  1.6 1.7 %copy-start = (bf16[8,24,48,128]{3,2,1,0:T(8,128)(2,1)S(1)}, bf16[8,24,48,128]{3,2,1,0:T(8,128)(2,1)}, u32[]{:S(2)}) copy-start(bf16[8,24,48,128]{3,2,1,0:T(8,128)(2,1)} %field.1) | copy-start | bytes 7077892
  3.2 0.7 %copy-start.1 = (bf16[24,48]{1,0:T(8,128)(2,1)S(1)}, bf16[24,48]{1,0:T(8,128)(2,1)}, u32[]{:S(2)}) copy-start(bf16[24,48]{1,0:T(8,128)(2,1)} %xf.1) | copy-start | bytes 6916

commit v2 on v1

v2 whole, which is shorter than its diff:
```python
import functools

import jax
import jax.numpy as jnp
from jax import lax
from jax.experimental import pallas as pl
from jax.experimental.pallas import tpu as pltpu
from jax.sharding import PartitionSpec as P

MESH = pl.DeviceIdType.MESH
F32 = jnp.float32
BF16 = jnp.bfloat16
NT = (((1,), (1,)), ((), ()))

NGX, NGZ, NGY = 16, 8, 2
XL, ZL = 24, 48
RI, RJ, RP, NS = 48, 48, 4, 8
ZG, ZZ = 10, 5
TOP = 32000.0
BIAS = 124.0
SHARE = 6
CH = 4
ROWS = XL * ZL // CH
FAR = (4, 12, 3, 11, 5, 13, 2, 10, 6, 14, 1, 9, 7, 15, 8)


def encode(value, inverse):
    whole = jnp.round(value * inverse)
    size = jnp.abs(whole)
    high = jnp.floor(size * (1.0 / 128.0))
    code = jnp.exp2(high - BIAS) * (1.0 + (size - 128.0 * high) * (1.0 / 128.0))
    return jnp.where(whole < 0.0, -code, code)


def decode(code):
    size = jnp.abs(code)
    high = jnp.floor(jnp.log2(size) + 0.002)
    whole = jnp.round(128.0 * (high + (BIAS - 1.0) + size * jnp.exp2(-high)))
    return jnp.where(code < 0.0, -whole, whole)


def scale_of(largest):
    unit = (largest * (1.01 / TOP)).astype(BF16).astype(F32)
    return jnp.maximum(unit, 2.0**-100)


def split(value):
    high = value.astype(BF16)
    return high, (value - high.astype(F32)).astype(BF16)


def kernel(field, xf_hbm, yf_hbm, sb_hbm, out, fbuf, xf, yf, sb, whi, wlo, mine, other, prt, tsum, xsend, xrecv, bd, asend, arecv,
           acc, d2, csend, owns, theirs, left_buf, right_buf, gsum, fin,
           f_sem, p_sem, es_sem, er_sem, xs_sem, xr_sem, as_sem, ar_sem, cs_sem, cr_sem, gs_sem, gr_sem, qs_sem, qr_sem):
    gx, gz, gy = lax.axis_index("gx"), lax.axis_index("gz"), lax.axis_index("gy")
    y_lo, z_at = gx // 8, gx % 8
    quad = y_lo * 2 + gy
    x_at, y_hi = gz // 2, gz % 2

    def to_gx(dd):
        return {"gx": (gx + dd) % NGX, "gz": gz, "gy": gy}

    def in_quad(dy, dc):
        return {"gx": (y_lo + dy) % 2 * 8 + z_at, "gz": gz, "gy": (gy + dc) % 2}

    def quad_of(dy, dc):
        return (y_lo + dy) % 2 * 2 + (gy + dc) % 2

    def charged(dx, dh):
        return {"gx": x_at // 2 * 8 + z_at, "gz": (x_at + dx) % 4 * 2 + (y_hi + dh) % 2, "gy": x_at % 2}

    params = [pltpu.make_async_copy(a, b, p_sem.at[k]) for k, (a, b) in enumerate(((xf_hbm, xf), (yf_hbm, yf), (sb_hbm, sb)))]
    for copy in params:
        copy.start()
    loads = []
    for c in range(CH):
        part = pl.ds(c * (XL // CH), XL // CH)
        loads.append(pltpu.make_async_copy(field.at[:, part], fbuf.at[:, part], f_sem.at[c]))
        loads[-1].start()

    barrier = pltpu.get_barrier_semaphore()

    for dd in range(1, NGX):
        pl.semaphore_signal(barrier, inc=1, device_id=to_gx(dd), device_id_type=MESH)
    for dy in range(2):
        pl.semaphore_signal(barrier, inc=1, device_id=in_quad(dy, 1), device_id_type=MESH)
    for b in range(2):
        @pl.when(2 * quad + b != gz)
        def _():
            for w in range(4):
                there = {"gx": w // 2 * 8 + z_at, "gz": 2 * quad + b, "gy": w % 2}
                pl.semaphore_signal(barrier, inc=1, device_id=there, device_id_type=MESH)

    for copy in params:
        copy.wait()

    x32 = xf[...].astype(F32)
    low = jnp.concatenate([x32[16:24], jnp.zeros((8, RI), F32)], axis=0)
    gap = jnp.zeros((16, 16), F32)
    xsend[...] = jnp.concatenate([x32[0:16], gap, low, gap], axis=1).astype(BF16)

    lane = lax.broadcasted_iota(jnp.int32, (RJ, 256), 1)
    q = lane & 7
    dest = (gx + ((lane >> 3) & 15)) & 15
    late = (q >= 3).astype(jnp.int32)
    jl = 3 * dest + q - 3 * late
    pick = (lax.broadcasted_iota(jnp.int32, (RJ, 256), 0) == jl) & (q < SHARE)
    spread = lax.dot_general(yf[...], pick.astype(F32).astype(BF16), (((0,), (0,)), ((), ())), preferred_element_type=F32)
    plane = (2 * (((lane >> 7) + gy) & 1) + late)[0:1]
    basis = sb[...]
    for s in range(NS):
        mix = jnp.zeros((1, 256), F32)
        for p in range(RP):
            mix = mix + jnp.where(plane == p, basis[p:p + 1, s:s + 1], 0.0)
        high, rest = split(spread * mix)
        whi[128 * s:128 * s + 128, :] = high
        wlo[128 * s:128 * s + 128, :] = rest

    exchanges = []
    for c in range(CH):
        loads[c].wait()
        left = jnp.concatenate(
            [fbuf[s, c * (XL // CH):(c + 1) * (XL // CH)].reshape(ROWS, 128) for s in range(NS)], axis=1)
        part = jnp.dot(left, whi[...], preferred_element_type=F32) + jnp.dot(left, wlo[...], preferred_element_type=F32)
        span = pl.ds(c * ROWS, ROWS)
        mine[span, :] = part[:, 0:128]
        other[span, :] = part[:, 128:256]
        exchanges.append(pltpu.make_async_remote_copy(
            other.at[span], prt.at[span], es_sem.at[c], er_sem.at[c], device_id=in_quad(0, 1), device_id_type=MESH))

    pl.semaphore_wait(barrier, NGX - 1 + 2 + NGZ - 1)
    for copy in exchanges:
        copy.start()
    xcopies = [
        pltpu.make_async_remote_copy(xsend, xrecv.at[dd], xs_sem.at[dd], xr_sem.at[dd], device_id=to_gx(dd), device_id_type=MESH)
        for dd in FAR
    ]
    for copy in xcopies:
        copy.start()

    largest = jnp.zeros((8, 128), F32)
    for c in range(CH):
        exchanges[c].wait_recv()
        span = pl.ds(c * ROWS, ROWS)
        total = mine[span, :] + prt[span, :]
        tsum[span, :] = total
        largest = jnp.maximum(largest, jnp.max(jnp.abs(total).reshape(ROWS // 8, 8, 128), axis=0))
    unit = scale_of(jnp.max(largest, keepdims=True))
    inverse = 1.0 / unit

    is_scale = lax.broadcasted_iota(jnp.int32, (NGX, 8, 128), 1) == SHARE

    def coded(zg):
        pieces = []
        for zz in range(ZZ):
            z = zg + ZG * zz
            pieces.append(tsum[pl.ds(z, XL, stride=ZL), :] if z < ZL else jnp.zeros((XL, 128), F32))
        pieces.append(jnp.zeros((8, 128), F32))
        tile = jnp.concatenate(pieces, axis=0).T
        return jnp.where(is_scale, unit.reshape(1, 1, 1), encode(tile, inverse).reshape(NGX, 8, 128))

    for m in range(ZG // 2):
        both = jnp.concatenate([coded(2 * m), coded(2 * m + 1)], axis=1)
        asend[:, 16 * m:16 * m + 16, :] = both.astype(BF16)

    acopies = {
        dd: pltpu.make_async_remote_copy(asend.at[dd], arecv.at[dd], as_sem.at[dd], ar_sem.at[dd], device_id=to_gx(dd), device_id_type=MESH)
        for dd in range(1, NGX)
    }
    for dd in FAR:
        acopies[dd].start()

    for copy in xcopies:
        copy.wait_recv()
    xrecv[0] = xsend[...]
    row = lax.broadcasted_iota(jnp.int32, (128, 256), 0)
    lane = lax.broadcasted_iota(jnp.int32, (128, 256), 1)
    slot = jnp.zeros((128, 256), jnp.int32)
    for zz in range(1, ZZ):
        slot = slot + (lane >= RI * zz).astype(jnp.int32)
    want = lane - RI * slot
    first = ((row == want) & (lane < RI * ZZ)).astype(F32).astype(BF16)
    second = ((row == want + 64) & (lane < RI * ZZ)).astype(F32).astype(BF16)
    everything = xrecv[...].reshape(NGX * 16, 128)
    upper = jnp.dot(everything, first, preferred_element_type=F32)
    lower = jnp.dot(everything, second, preferred_element_type=F32)
    column = slot[0:XL]
    for dd in range(NGX):
        block = jnp.concatenate([upper[16 * dd:16 * dd + 16], lower[16 * dd:16 * dd + 8]], axis=0)
        stack = [jnp.where(column == zz, block, 0.0) for zz in range(ZZ)] + [jnp.zeros((8, 256), F32)]
        bd[128 * dd:128 * dd + 128, :] = jnp.concatenate(stack, axis=0).astype(BF16)

    for k in range(NGX // 2):
        sides = []
        for dd in (2 * k, 2 * k + 1):
            if dd:
                acopies[dd].wait_recv()
            held = (arecv if dd else asend)[dd].astype(F32)
            sides.append(decode(held) * held[SHARE:SHARE + 1, :])
        high, rest = split(jnp.concatenate(sides, axis=1))
        product = jnp.dot(jnp.concatenate([high, rest], axis=0), bd[256 * k:256 * k + 256, :], preferred_element_type=F32)
        if k == 0:
            acc[...] = product
        else:
            acc[...] += product

    core = acc[0:80, :] + acc[80:160, :]
    for zz in range(ZZ):
        d2[80 * zz:80 * zz + 80, 0:RI] = core[:, RI * zz:RI * zz + RI]
    rows = jnp.concatenate([d2[pl.ds(c, ZL, stride=8), :][:, 0:RI] for c in range(SHARE)], axis=1)
    unit = scale_of(jnp.max(jnp.abs(rows), keepdims=True))
    words = jnp.concatenate([encode(rows, 1.0 / unit), jnp.broadcast_to(unit, (ZL, 96))], axis=1)
    csend[...] = words.astype(BF16)

    ccopies = []
    for dx, dh in ((2, 1), (1, 1), (3, 1), (0, 1), (2, 0), (1, 0), (3, 0)):
        k = 2 * dx + dh
        ccopies.append(pltpu.make_async_remote_copy(
            csend, theirs.at[4 * y_hi + quad], cs_sem.at[k], cr_sem.at[4 + 4 * y_hi + quad], device_id=charged(dx, dh), device_id_type=MESH))
    for dy, dc in ((1, 1), (1, 0), (0, 1)):
        ccopies.append(pltpu.make_async_remote_copy(
            csend, owns.at[quad], cs_sem.at[8 + 2 * dy + dc], cr_sem.at[quad], device_id=in_quad(dy, dc), device_id_type=MESH))
    for copy in ccopies:
        copy.start()
    owns[quad] = csend[...]
    real = lax.broadcasted_iota(jnp.int32, (ZL, 384), 1) < SHARE * RI

    def opened(words):
        held = words.astype(F32)
        return split(jnp.where(real, decode(held) * held[:, 288:289], 0.0))

    for dy, dc in ((0, 1), (1, 0), (1, 1)):
        w = quad_of(dy, dc)
        pltpu.make_async_copy(owns.at[w], owns.at[w], cr_sem.at[w]).wait()
    for w in range(4):
        left_buf[0:ZL, 384 * w:384 * w + 384], left_buf[ZL:2 * ZL, 384 * w:384 * w + 384] = opened(owns[w])
    for b in range(2):
        @pl.when(2 * quad + b != gz)
        def _():
            for w in range(4):
                k = 4 * b + w
                pltpu.make_async_copy(theirs.at[k], theirs.at[k], cr_sem.at[4 + k]).wait()

        @pl.when(2 * quad + b == gz)
        def _():
            for w in range(4):
                theirs[4 * b + w] = owns[w]

        for w in range(4):
            at = pl.ds(384 * w, 384)
            right_buf[ZL * b:ZL * b + ZL, at], right_buf[128 + ZL * b:128 + ZL * b + ZL, at] = opened(theirs[4 * b + w])
    right_buf[96:128, :] = jnp.zeros((32, 1536), BF16)
    right_buf[224:256, :] = jnp.zeros((32, 1536), BF16)
    gram = lax.dot_general(left_buf[...], right_buf[...], NT, preferred_element_type=F32)
    gram = (gram[0:ZL] + gram[ZL:2 * ZL]) * (1.0 / (RI * RJ * RP))
    gsum[z_at] = gram[:, 0:128] + gram[:, 128:256]

    gcopies = [
        pltpu.make_async_remote_copy(
            gsum.at[z_at], gsum.at[z_at], gs_sem.at[dz], gr_sem.at[z_at],
            device_id={"gx": y_lo * 8 + (z_at + dz) % 8, "gz": gz, "gy": gy}, device_id_type=MESH)
        for dz in (4, 3, 5, 2, 6, 1, 7)
    ]
    for copy in gcopies:
        copy.start()
    for dz in (7, 1, 6, 2, 5, 3, 4):
        w = (z_at + dz) % 8
        pltpu.make_async_copy(gsum.at[w], gsum.at[w], gr_sem.at[w]).wait()
    total = gsum[0]
    for k in range(1, 8):
        total = total + gsum[k]
    fin[quad] = total

    qcopies = [
        pltpu.make_async_remote_copy(
            fin.at[quad], fin.at[quad], qs_sem.at[2 * dy + dc], qr_sem.at[quad], device_id=in_quad(dy, dc), device_id_type=MESH)
        for dy, dc in ((1, 1), (1, 0), (0, 1))
    ]
    for copy in qcopies:
        copy.start()
    for dy, dc in ((0, 1), (1, 0), (1, 1)):
        w = quad_of(dy, dc)
        pltpu.make_async_copy(fin.at[w], fin.at[w], qr_sem.at[w]).wait()
    out[...] = jnp.concatenate([fin[w][:, 0:96] for w in range(4)], axis=1)

    for copy in xcopies + exchanges + list(acopies.values()) + ccopies + gcopies + qcopies:
        copy.wait_send()


def body(field, x_factor, y_factor, species_basis_matrix):
    vmem = pl.BlockSpec(memory_space=pltpu.VMEM)
    dma = pltpu.SemaphoreType.DMA
    return pl.pallas_call(
        kernel,
        out_shape=jax.ShapeDtypeStruct((ZL, NGZ * ZL), F32),
        in_specs=[pl.BlockSpec(memory_space=pltpu.HBM)] * 4,
        out_specs=vmem,
        scratch_shapes=[
            pltpu.VMEM((NS, XL, ZL, 128), BF16),
            pltpu.VMEM((XL, RI), BF16),
            pltpu.VMEM((RJ, 128), BF16),
            pltpu.VMEM((RP, NS), F32),
            pltpu.VMEM((1024, 256), BF16),
            pltpu.VMEM((1024, 256), BF16),
            pltpu.VMEM((XL * ZL, 128), F32),
            pltpu.VMEM((XL * ZL, 128), F32),
            pltpu.VMEM((XL * ZL, 128), F32),
            pltpu.VMEM((XL * ZL, 128), F32),
            pltpu.VMEM((16, 128), BF16),
            pltpu.VMEM((NGX, 16, 128), BF16),
            pltpu.VMEM((NGX * 128, 256), BF16),
            pltpu.VMEM((NGX, 80, 128), BF16),
            pltpu.VMEM((NGX, 80, 128), BF16),
            pltpu.VMEM((160, 256), F32),
            pltpu.VMEM((400, 128), F32),
            pltpu.VMEM((ZL, 384), BF16),
            pltpu.VMEM((4, ZL, 384), BF16),
            pltpu.VMEM((8, ZL, 384), BF16),
            pltpu.VMEM((96, 1536), BF16),
            pltpu.VMEM((256, 1536), BF16),
            pltpu.VMEM((8, ZL, 128), F32),
            pltpu.VMEM((4, ZL, 128), F32),
            dma((CH,)), dma((3,)), dma((CH,)), dma((CH,)), dma((NGX,)), dma((NGX,)), dma((NGX,)), dma((NGX,)),
            dma((12,)), dma((12,)), dma((8,)), dma((8,)), dma((4,)), dma((4,)),
        ],
        compiler_params=pltpu.CompilerParams(collective_id=0, has_side_effects=True, vmem_limit_bytes=56 * 1024 * 1024),
    )(field, x_factor, y_factor.T, species_basis_matrix.T)


def solution(mesh):
    placed = (P(None, "gx", "gz", "gy"), P("gx", None), P("gy", None), P())
    return jax.shard_map(body, mesh=mesh, in_specs=placed, out_specs=P("gz", None), check_vma=False)
```

time: 51.1 us -> 44.8 us (0.88)
  Pallas kernels: 46.3 us -> 43.1 us
  local copies, waits for them, and re-layouts: 4.57 us -> 1.52 us
    pallas_call x1, Pallas kernels: 46.3 us -> 43.1 us  [body(): pl.pallas_call(kernel, out_shape=jax.ShapeDtypeStruct((ZL, NGZ * ZL), F32...]
    unnamed x7 -> x1, local copies, waits for them, and re-layouts: 4.57 us -> 1.52 us
where the time goes in v2:
time: 44.8 us; the launch traced here: 44.6 us
  Pallas kernels  43.1 us (96%)
  local copies, waits for them, and re-layouts  1.52 us (3%)
    pallas_call x1, Pallas kernels, body(): pl.pallas_call(kernel, out_shape=jax.ShapeDtypeStruct((ZL, NGZ * ZL), F32...  43.1 us
    unnamed x1, local copies, waits for them, and re-layouts  1.52 us

profile of v2, /device:TPU:1, one launch (start us, length us, event | category | flops | bytes accessed | tf_op | source)
XLA Modules:
  0.0 44.6 jit_solution(11125952114949054373)
XLA Ops:
  0.0 43.1 %shard_map.46 = f32[48,384]{1,0:T(8,128)} custom-call(bf16[8,24,48,128]{3,2,1,0:T(8,128)(2,1)} %field.1, bf16[24,48]{1,0:T(8,128)(2,1)} %xf_hbm.1, bf16[48,128]{1,0:T(8,128)(2,1)} %bitcast.2, f32[4,8]{1,0:T(4,128)} %bitcast.3), custom_call_target="tpu_custom_call" | custom-call | tf_op jit(solution)/shard_map/pallas_call | solution.py:293
  43.1 1.5 %copy.6 = f32[48,384]{1,0:T(8,128)} copy(f32[48,384]{1,0:T(8,128)} %shard_map.46) | data formatting | bytes 147456

commit v3 on v2

--- a/solution.py
+++ b/solution.py
@@ -69,18 +69,9 @@
     def charged(dx, dh):
         return {"gx": x_at // 2 * 8 + z_at, "gz": (x_at + dx) % 4 * 2 + (y_hi + dh) % 2, "gy": x_at % 2}
 
-    params = [pltpu.make_async_copy(a, b, p_sem.at[k]) for k, (a, b) in enumerate(((xf_hbm, xf), (yf_hbm, yf), (sb_hbm, sb)))]
-    for copy in params:
-        copy.start()
-    loads = []
-    for c in range(CH):
-        part = pl.ds(c * (XL // CH), XL // CH)
-        loads.append(pltpu.make_async_copy(field.at[:, part], fbuf.at[:, part], f_sem.at[c]))
-        loads[-1].start()
-
     barrier = pltpu.get_barrier_semaphore()
 
-    for dd in range(1, NGX):
+    for dd in FAR:
         pl.semaphore_signal(barrier, inc=1, device_id=to_gx(dd), device_id_type=MESH)
     for dy in range(2):
         pl.semaphore_signal(barrier, inc=1, device_id=in_quad(dy, 1), device_id_type=MESH)
@@ -90,6 +81,15 @@
             for w in range(4):
                 there = {"gx": w // 2 * 8 + z_at, "gz": 2 * quad + b, "gy": w % 2}
                 pl.semaphore_signal(barrier, inc=1, device_id=there, device_id_type=MESH)
+
+    params = [pltpu.make_async_copy(a, b, p_sem.at[k]) for k, (a, b) in enumerate(((xf_hbm, xf), (yf_hbm, yf), (sb_hbm, sb)))]
+    for copy in params:
+        copy.start()
+    loads = []
+    for c in range(CH):
+        part = pl.ds(c * (XL // CH), XL // CH)
+        loads.append(pltpu.make_async_copy(field.at[:, part], fbuf.at[:, part], f_sem.at[c]))
+        loads[-1].start()
 
     for copy in params:
         copy.wait()
@@ -116,6 +116,7 @@
         whi[128 * s:128 * s + 128, :] = high
         wlo[128 * s:128 * s + 128, :] = rest
 
+    spare = lax.broadcasted_iota(jnp.int32, (ROWS, 128), 1) & 7
     exchanges = []
     for c in range(CH):
         loads[c].wait()
@@ -124,7 +125,8 @@
         part = jnp.dot(left, whi[...], preferred_element_type=F32) + jnp.dot(left, wlo[...], preferred_element_type=F32)
         span = pl.ds(c * ROWS, ROWS)
         mine[span, :] = part[:, 0:128]
-        other[span, :] = part[:, 128:256]
+        unit = scale_of(jnp.max(jnp.abs(part[:, 128:256]), keepdims=True))
+        other[span, :] = jnp.where(spare == SHARE, unit, encode(part[:, 128:256], 1.0 / unit)).astype(BF16)
         exchanges.append(pltpu.make_async_remote_copy(
             other.at[span], prt.at[span], es_sem.at[c], er_sem.at[c], device_id=in_quad(0, 1), device_id_type=MESH))
 
@@ -142,13 +144,14 @@
     for c in range(CH):
         exchanges[c].wait_recv()
         span = pl.ds(c * ROWS, ROWS)
-        total = mine[span, :] + prt[span, :]
+        came = prt[span, :].astype(F32)
+        total = mine[span, :] + jnp.where(spare < SHARE, decode(came) * came[0:1, SHARE:SHARE + 1], 0.0)
         tsum[span, :] = total
         largest = jnp.maximum(largest, jnp.max(jnp.abs(total).reshape(ROWS // 8, 8, 128), axis=0))
     unit = scale_of(jnp.max(largest, keepdims=True))
     inverse = 1.0 / unit
 
-    is_scale = lax.broadcasted_iota(jnp.int32, (NGX, 8, 128), 1) == SHARE
+    line = lax.broadcasted_iota(jnp.int32, (NGX, 8, 128), 1)
 
     def coded(zg):
         pieces = []
@@ -156,12 +159,17 @@
             z = zg + ZG * zz
             pieces.append(tsum[pl.ds(z, XL, stride=ZL), :] if z < ZL else jnp.zeros((XL, 128), F32))
         pieces.append(jnp.zeros((8, 128), F32))
-        tile = jnp.concatenate(pieces, axis=0).T
-        return jnp.where(is_scale, unit.reshape(1, 1, 1), encode(tile, inverse).reshape(NGX, 8, 128))
-
-    for m in range(ZG // 2):
-        both = jnp.concatenate([coded(2 * m), coded(2 * m + 1)], axis=1)
-        asend[:, 16 * m:16 * m + 16, :] = both.astype(BF16)
+        return encode(jnp.concatenate(pieces, axis=0).T, inverse).reshape(NGX, 8, 128)
+
+    tails = (coded(8), coded(9))
+
+    def packed(zg):
+        if zg < 6:
+            return jnp.where(line < SHARE, coded(zg), pltpu.roll(tails[zg // 3], 6 - 2 * (zg % 3), axis=1))
+        return jnp.where(line == SHARE, unit.reshape(1, 1, 1), coded(zg))
+
+    for m in range(4):
+        asend[:, 16 * m:16 * m + 16, :] = jnp.concatenate([packed(2 * m), packed(2 * m + 1)], axis=1).astype(BF16)
 
     acopies = {
         dd: pltpu.make_async_remote_copy(asend.at[dd], arecv.at[dd], as_sem.at[dd], ar_sem.at[dd], device_id=to_gx(dd), device_id_type=MESH)
@@ -190,13 +198,19 @@
         stack = [jnp.where(column == zz, block, 0.0) for zz in range(ZZ)] + [jnp.zeros((8, 256), F32)]
         bd[128 * dd:128 * dd + 128, :] = jnp.concatenate(stack, axis=0).astype(BF16)
 
+    eight = lax.broadcasted_iota(jnp.int32, (8, 128), 0)
     for k in range(NGX // 2):
         sides = []
         for dd in (2 * k, 2 * k + 1):
             if dd:
                 acopies[dd].wait_recv()
             held = (arecv if dd else asend)[dd].astype(F32)
-            sides.append(decode(held) * held[SHARE:SHARE + 1, :])
+            value = decode(held) * held[48 + SHARE:48 + SHARE + 1, :]
+            tails = []
+            for t in range(2):
+                a, b, c = (pltpu.roll(value[24 * t + 8 * n:24 * t + 8 * n + 8], 2 * n + 2, axis=0) for n in range(3))
+                tails.append(jnp.where(eight < 2, a, jnp.where(eight < 4, b, c)))
+            sides.append(jnp.concatenate([value] + tails, axis=0))
         high, rest = split(jnp.concatenate(sides, axis=1))
         product = jnp.dot(jnp.concatenate([high, rest], axis=0), bd[256 * k:256 * k + 256, :], preferred_element_type=F32)
         if k == 0:
@@ -209,8 +223,9 @@
         d2[80 * zz:80 * zz + 80, 0:RI] = core[:, RI * zz:RI * zz + RI]
     rows = jnp.concatenate([d2[pl.ds(c, ZL, stride=8), :][:, 0:RI] for c in range(SHARE)], axis=1)
     unit = scale_of(jnp.max(jnp.abs(rows), keepdims=True))
-    words = jnp.concatenate([encode(rows, 1.0 / unit), jnp.broadcast_to(unit, (ZL, 96))], axis=1)
-    csend[...] = words.astype(BF16)
+    words = encode(rows, 1.0 / unit)
+    rest = [words[16 * k:16 * k + 16, 256:288] for k in range(3)] + [jnp.broadcast_to(unit, (16, 32))]
+    csend[...] = jnp.concatenate([words[:, 0:128], words[:, 128:256], jnp.concatenate(rest, axis=1)], axis=0).astype(BF16)
 
     ccopies = []
     for dx, dh in ((2, 1), (1, 1), (3, 1), (0, 1), (2, 0), (1, 0), (3, 0)):
@@ -223,17 +238,22 @@
     for copy in ccopies:
         copy.start()
     owns[quad] = csend[...]
-    real = lax.broadcasted_iota(jnp.int32, (ZL, 384), 1) < SHARE * RI
-
-    def opened(words):
-        held = words.astype(F32)
-        return split(jnp.where(real, decode(held) * held[:, 288:289], 0.0))
+
+    def opened(pieces, buf, at, low):
+        rests = []
+        for w in range(4):
+            held = pieces[w].astype(F32)
+            value = decode(held) * held[96:97, 96:97]
+            for k in range(2):
+                lanes = pl.ds(256 * w + 128 * k, 128)
+                buf[at:at + ZL, lanes], buf[low:low + ZL, lanes] = split(value[ZL * k:ZL * k + ZL])
+            rests.append(jnp.concatenate([value[96:112, 32 * k:32 * k + 32] for k in range(3)], axis=0))
+        buf[at:at + ZL, 1024:1152], buf[low:low + ZL, 1024:1152] = split(jnp.concatenate(rests, axis=1))
 
     for dy, dc in ((0, 1), (1, 0), (1, 1)):
         w = quad_of(dy, dc)
         pltpu.make_async_copy(owns.at[w], owns.at[w], cr_sem.at[w]).wait()
-    for w in range(4):
-        left_buf[0:ZL, 384 * w:384 * w + 384], left_buf[ZL:2 * ZL, 384 * w:384 * w + 384] = opened(owns[w])
+    opened([owns[w] for w in range(4)], left_buf, 0, ZL)
     for b in range(2):
         @pl.when(2 * quad + b != gz)
         def _():
@@ -246,14 +266,15 @@
             for w in range(4):
                 theirs[4 * b + w] = owns[w]
 
-        for w in range(4):
-            at = pl.ds(384 * w, 384)
-            right_buf[ZL * b:ZL * b + ZL, at], right_buf[128 + ZL * b:128 + ZL * b + ZL, at] = opened(theirs[4 * b + w])
-    right_buf[96:128, :] = jnp.zeros((32, 1536), BF16)
-    right_buf[224:256, :] = jnp.zeros((32, 1536), BF16)
+        opened([theirs[4 * b + w] for w in range(4)], right_buf, ZL * b, 128 + ZL * b)
+    right_buf[96:128, :] = jnp.zeros((32, 1152), BF16)
+    right_buf[224:256, :] = jnp.zeros((32, 1152), BF16)
     gram = lax.dot_general(left_buf[...], right_buf[...], NT, preferred_element_type=F32)
     gram = (gram[0:ZL] + gram[ZL:2 * ZL]) * (1.0 / (RI * RJ * RP))
-    gsum[z_at] = gram[:, 0:128] + gram[:, 128:256]
+    gram = gram[:, 0:128] + gram[:, 128:256]
+    unit = scale_of(jnp.max(jnp.abs(gram), keepdims=True))
+    beyond = lax.broadcasted_iota(jnp.int32, (ZL, 128), 1) >= 96
+    gsum[z_at] = jnp.where(beyond, unit, encode(gram, 1.0 / unit)).astype(BF16)
 
     gcopies = [
         pltpu.make_async_remote_copy(
@@ -266,9 +287,10 @@
     for dz in (7, 1, 6, 2, 5, 3, 4):
         w = (z_at + dz) % 8
         pltpu.make_async_copy(gsum.at[w], gsum.at[w], gr_sem.at[w]).wait()
-    total = gsum[0]
-    for k in range(1, 8):
-        total = total + gsum[k]
+    total = jnp.zeros((ZL, 128), F32)
+    for k in range(8):
+        held = gsum[k].astype(F32)
+        total = total + decode(held) * held[:, 96:97]
     fin[quad] = total
 
     qcopies = [
@@ -303,22 +325,22 @@
             pltpu.VMEM((1024, 256), BF16),
             pltpu.VMEM((1024, 256), BF16),
             pltpu.VMEM((XL * ZL, 128), F32),
-            pltpu.VMEM((XL * ZL, 128), F32),
-            pltpu.VMEM((XL * ZL, 128), F32),
+            pltpu.VMEM((XL * ZL, 128), BF16),
+            pltpu.VMEM((XL * ZL, 128), BF16),
             pltpu.VMEM((XL * ZL, 128), F32),
             pltpu.VMEM((16, 128), BF16),
             pltpu.VMEM((NGX, 16, 128), BF16),
             pltpu.VMEM((NGX * 128, 256), BF16),
-            pltpu.VMEM((NGX, 80, 128), BF16),
-            pltpu.VMEM((NGX, 80, 128), BF16),
+            pltpu.VMEM((NGX, 64, 128), BF16),
+            pltpu.VMEM((NGX, 64, 128), BF16),
             pltpu.VMEM((160, 256), F32),
             pltpu.VMEM((400, 128), F32),
-            pltpu.VMEM((ZL, 384), BF16),
-            pltpu.VMEM((4, ZL, 384), BF16),
-            pltpu.VMEM((8, ZL, 384), BF16),
-            pltpu.VMEM((96, 1536), BF16),
-            pltpu.VMEM((256, 1536), BF16),
-            pltpu.VMEM((8, ZL, 128), F32),
+            pltpu.VMEM((112, 128), BF16),
+            pltpu.VMEM((4, 112, 128), BF16),
+            pltpu.VMEM((8, 112, 128), BF16),
+            pltpu.VMEM((96, 1152), BF16),
+            pltpu.VMEM((256, 1152), BF16),
+            pltpu.VMEM((8, ZL, 128), BF16),
             pltpu.VMEM((4, ZL, 128), F32),
             dma((CH,)), dma((3,)), dma((CH,)), dma((CH,)), dma((NGX,)), dma((NGX,)), dma((NGX,)), dma((NGX,)),
             dma((12,)), dma((12,)), dma((8,)), dma((8,)), dma((4,)), dma((4,)),

time: 44.8 us -> 41.9 us (0.935)
  Pallas kernels: 43.1 us -> 40.2 us
    pallas_call x1, Pallas kernels: 43.1 us -> 40.2 us  [body(): pl.pallas_call(kernel, out_shape=jax.ShapeDtypeStruct((ZL, NGZ * ZL), F32...]
where the time goes in v3:
time: 41.9 us; the launch traced here: 41.7 us
  Pallas kernels  40.2 us (96%)
  local copies, waits for them, and re-layouts  1.52 us (4%)
    pallas_call x1, Pallas kernels, body(): pl.pallas_call(kernel, out_shape=jax.ShapeDtypeStruct((ZL, NGZ * ZL), F32...  40.2 us
    unnamed x1, local copies, waits for them, and re-layouts  1.52 us

profile of v3, /device:TPU:1, one launch (start us, length us, event | category | flops | bytes accessed | tf_op | source)
XLA Modules:
  0.0 41.7 jit_solution(2940060121006055597)
XLA Ops:
  0.0 40.2 %shard_map.46 = f32[48,384]{1,0:T(8,128)} custom-call(bf16[8,24,48,128]{3,2,1,0:T(8,128)(2,1)} %field.1, bf16[24,48]{1,0:T(8,128)(2,1)} %xf_hbm.1, bf16[48,128]{1,0:T(8,128)(2,1)} %bitcast.2, f32[4,8]{1,0:T(4,128)} %bitcast.3), custom_call_target="tpu_custom_call" | custom-call | tf_op jit(solution)/shard_map/pallas_call | solution.py:315
  40.2 1.5 %copy.6 = f32[48,384]{1,0:T(8,128)} copy(f32[48,384]{1,0:T(8,128)} %shard_map.46) | data formatting | bytes 147456

commit v4 on v3

--- a/solution.py
+++ b/solution.py
@@ -9,6 +9,7 @@
 
 MESH = pl.DeviceIdType.MESH
 F32 = jnp.float32
+I32 = jnp.int32
 BF16 = jnp.bfloat16
 NT = (((1,), (1,)), ((), ()))
 
@@ -24,6 +25,14 @@
 FAR = (4, 12, 3, 11, 5, 13, 2, 10, 6, 14, 1, 9, 7, 15, 8)
 
 
+def rem(number, by):
+    return lax.rem(number, I32(by))
+
+
+def div(number, by):
+    return lax.div(number, I32(by))
+
+
 def encode(value, inverse):
     whole = jnp.round(value * inverse)
     size = jnp.abs(whole)
@@ -49,52 +58,52 @@
     return high, (value - high.astype(F32)).astype(BF16)
 
 
-def kernel(field, xf_hbm, yf_hbm, sb_hbm, out, fbuf, xf, yf, sb, whi, wlo, mine, other, prt, tsum, xsend, xrecv, bd, asend, arecv,
+def kernel(field, factors, out, fbuf, whi, wlo, mine, other, prt, tsum, xsend, xrecv, bd, asend, arecv,
            acc, d2, csend, owns, theirs, left_buf, right_buf, gsum, fin,
-           f_sem, p_sem, es_sem, er_sem, xs_sem, xr_sem, as_sem, ar_sem, cs_sem, cr_sem, gs_sem, gr_sem, qs_sem, qr_sem):
+           f_sem, es_sem, er_sem, xs_sem, xr_sem, as_sem, ar_sem, cs_sem, cr_sem, gs_sem, gr_sem, qs_sem, qr_sem):
     gx, gz, gy = lax.axis_index("gx"), lax.axis_index("gz"), lax.axis_index("gy")
-    y_lo, z_at = gx // 8, gx % 8
+    y_lo, z_at = div(gx, 8), rem(gx, 8)
     quad = y_lo * 2 + gy
-    x_at, y_hi = gz // 2, gz % 2
+    x_at, y_hi = div(gz, 2), rem(gz, 2)
 
     def to_gx(dd):
-        return {"gx": (gx + dd) % NGX, "gz": gz, "gy": gy}
+        return {"gx": rem(gx + dd, NGX), "gz": gz, "gy": gy}
 
     def in_quad(dy, dc):
-        return {"gx": (y_lo + dy) % 2 * 8 + z_at, "gz": gz, "gy": (gy + dc) % 2}
+        return {"gx": rem(y_lo + dy, 2) * 8 + z_at, "gz": gz, "gy": rem(gy + dc, 2)}
 
     def quad_of(dy, dc):
-        return (y_lo + dy) % 2 * 2 + (gy + dc) % 2
+        return rem(y_lo + dy, 2) * 2 + rem(gy + dc, 2)
 
     def charged(dx, dh):
-        return {"gx": x_at // 2 * 8 + z_at, "gz": (x_at + dx) % 4 * 2 + (y_hi + dh) % 2, "gy": x_at % 2}
+        return {"gx": div(x_at, 2) * 8 + z_at, "gz": rem(x_at + dx, 4) * 2 + rem(y_hi + dh, 2), "gy": rem(x_at, 2)}
+
+    loads = []
+    for c in range(CH):
+        part = pl.ds(c * (NS // CH), NS // CH)
+        loads.append(pltpu.make_async_copy(field.at[part], fbuf.at[part], f_sem.at[c]))
+        loads[-1].start()
 
     barrier = pltpu.get_barrier_semaphore()
 
-    for dd in FAR:
-        pl.semaphore_signal(barrier, inc=1, device_id=to_gx(dd), device_id_type=MESH)
-    for dy in range(2):
-        pl.semaphore_signal(barrier, inc=1, device_id=in_quad(dy, 1), device_id_type=MESH)
+    def greet(there):
+        pl.semaphore_signal(barrier, inc=1, device_id=there, device_id_type=MESH)
+
+    for dd in FAR[0:4]:
+        greet(to_gx(dd))
     for b in range(2):
         @pl.when(2 * quad + b != gz)
         def _():
             for w in range(4):
-                there = {"gx": w // 2 * 8 + z_at, "gz": 2 * quad + b, "gy": w % 2}
-                pl.semaphore_signal(barrier, inc=1, device_id=there, device_id_type=MESH)
-
-    params = [pltpu.make_async_copy(a, b, p_sem.at[k]) for k, (a, b) in enumerate(((xf_hbm, xf), (yf_hbm, yf), (sb_hbm, sb)))]
-    for copy in params:
-        copy.start()
-    loads = []
-    for c in range(CH):
-        part = pl.ds(c * (XL // CH), XL // CH)
-        loads.append(pltpu.make_async_copy(field.at[:, part], fbuf.at[:, part], f_sem.at[c]))
-        loads[-1].start()
-
-    for copy in params:
-        copy.wait()
-
-    x32 = xf[...].astype(F32)
+                greet({"gx": w // 2 * 8 + z_at, "gz": 2 * quad + b, "gy": w % 2})
+
+    for dd in FAR[4:]:
+        greet(to_gx(dd))
+    for dy in range(2):
+        greet(in_quad(dy, 1))
+
+
+    x32 = factors[RJ:RJ + XL, 0:RI]
     low = jnp.concatenate([x32[16:24], jnp.zeros((8, RI), F32)], axis=0)
     gap = jnp.zeros((16, 16), F32)
     xsend[...] = jnp.concatenate([x32[0:16], gap, low, gap], axis=1).astype(BF16)
@@ -105,9 +114,9 @@
     late = (q >= 3).astype(jnp.int32)
     jl = 3 * dest + q - 3 * late
     pick = (lax.broadcasted_iota(jnp.int32, (RJ, 256), 0) == jl) & (q < SHARE)
-    spread = lax.dot_general(yf[...], pick.astype(F32).astype(BF16), (((0,), (0,)), ((), ())), preferred_element_type=F32)
+    spread = lax.dot_general(factors[0:RJ, :].astype(BF16), pick.astype(F32).astype(BF16), (((0,), (0,)), ((), ())), preferred_element_type=F32)
     plane = (2 * (((lane >> 7) + gy) & 1) + late)[0:1]
-    basis = sb[...]
+    basis = factors[RJ + XL:RJ + XL + RP, 0:NS]
     for s in range(NS):
         mix = jnp.zeros((1, 256), F32)
         for p in range(RP):
@@ -117,22 +126,22 @@
         wlo[128 * s:128 * s + 128, :] = rest
 
     spare = lax.broadcasted_iota(jnp.int32, (ROWS, 128), 1) & 7
+    for load in loads:
+        load.wait()
+    left = jnp.concatenate([fbuf[s].reshape(XL * ZL, 128) for s in range(NS)], axis=1)
+    part = jnp.dot(left, whi[...], preferred_element_type=F32) + jnp.dot(left, wlo[...], preferred_element_type=F32)
+    mine[...] = part[:, 0:128]
+    pl.semaphore_wait(barrier, NGX - 1 + 2 + NGZ - 1)
     exchanges = []
     for c in range(CH):
-        loads[c].wait()
-        left = jnp.concatenate(
-            [fbuf[s, c * (XL // CH):(c + 1) * (XL // CH)].reshape(ROWS, 128) for s in range(NS)], axis=1)
-        part = jnp.dot(left, whi[...], preferred_element_type=F32) + jnp.dot(left, wlo[...], preferred_element_type=F32)
         span = pl.ds(c * ROWS, ROWS)
-        mine[span, :] = part[:, 0:128]
-        unit = scale_of(jnp.max(jnp.abs(part[:, 128:256]), keepdims=True))
-        other[span, :] = jnp.where(spare == SHARE, unit, encode(part[:, 128:256], 1.0 / unit)).astype(BF16)
+        away = part[c * ROWS:c * ROWS + ROWS, 128:256]
+        unit = scale_of(jnp.max(jnp.abs(away), keepdims=True))
+        other[span, :] = jnp.where(spare == SHARE, unit, encode(away, 1.0 / unit)).astype(BF16)
         exchanges.append(pltpu.make_async_remote_copy(
             other.at[span], prt.at[span], es_sem.at[c], er_sem.at[c], device_id=in_quad(0, 1), device_id_type=MESH))
-
-    pl.semaphore_wait(barrier, NGX - 1 + 2 + NGZ - 1)
-    for copy in exchanges:
-        copy.start()
+        exchanges[-1].start()
+
     xcopies = [
         pltpu.make_async_remote_copy(xsend, xrecv.at[dd], xs_sem.at[dd], xr_sem.at[dd], device_id=to_gx(dd), device_id_type=MESH)
         for dd in FAR
@@ -237,6 +246,8 @@
             csend, owns.at[quad], cs_sem.at[8 + 2 * dy + dc], cr_sem.at[quad], device_id=in_quad(dy, dc), device_id_type=MESH))
     for copy in ccopies:
         copy.start()
+    for copy in xcopies + exchanges + list(acopies.values()):
+        copy.wait_send()
     owns[quad] = csend[...]
 
     def opened(pieces, buf, at, low):
@@ -246,15 +257,17 @@
             value = decode(held) * held[96:97, 96:97]
             for k in range(2):
                 lanes = pl.ds(256 * w + 128 * k, 128)
-                buf[at:at + ZL, lanes], buf[low:low + ZL, lanes] = split(value[ZL * k:ZL * k + ZL])
+                buf[pl.ds(at, ZL), lanes], buf[pl.ds(low, ZL), lanes] = split(value[ZL * k:ZL * k + ZL])
             rests.append(jnp.concatenate([value[96:112, 32 * k:32 * k + 32] for k in range(3)], axis=0))
-        buf[at:at + ZL, 1024:1152], buf[low:low + ZL, 1024:1152] = split(jnp.concatenate(rests, axis=1))
+        buf[pl.ds(at, ZL), 1024:1152], buf[pl.ds(low, ZL), 1024:1152] = split(jnp.concatenate(rests, axis=1))
 
     for dy, dc in ((0, 1), (1, 0), (1, 1)):
         w = quad_of(dy, dc)
         pltpu.make_async_copy(owns.at[w], owns.at[w], cr_sem.at[w]).wait()
     opened([owns[w] for w in range(4)], left_buf, 0, ZL)
-    for b in range(2):
+    for near in range(2):
+        b = rem(y_hi + near, 2)
+
         @pl.when(2 * quad + b != gz)
         def _():
             for w in range(4):
@@ -266,7 +279,8 @@
             for w in range(4):
                 theirs[4 * b + w] = owns[w]
 
-        opened([theirs[4 * b + w] for w in range(4)], right_buf, ZL * b, 128 + ZL * b)
+        at = pl.multiple_of(ZL * b, 16)
+        opened([theirs[4 * b + w] for w in range(4)], right_buf, at, at + 128)
     right_buf[96:128, :] = jnp.zeros((32, 1152), BF16)
     right_buf[224:256, :] = jnp.zeros((32, 1152), BF16)
     gram = lax.dot_general(left_buf[...], right_buf[...], NT, preferred_element_type=F32)
@@ -279,13 +293,15 @@
     gcopies = [
         pltpu.make_async_remote_copy(
             gsum.at[z_at], gsum.at[z_at], gs_sem.at[dz], gr_sem.at[z_at],
-            device_id={"gx": y_lo * 8 + (z_at + dz) % 8, "gz": gz, "gy": gy}, device_id_type=MESH)
+            device_id={"gx": y_lo * 8 + rem(z_at + dz, 8), "gz": gz, "gy": gy}, device_id_type=MESH)
         for dz in (4, 3, 5, 2, 6, 1, 7)
     ]
     for copy in gcopies:
         copy.start()
+    for copy in ccopies:
+        copy.wait_send()
     for dz in (7, 1, 6, 2, 5, 3, 4):
-        w = (z_at + dz) % 8
+        w = rem(z_at + dz, 8)
         pltpu.make_async_copy(gsum.at[w], gsum.at[w], gr_sem.at[w]).wait()
     total = jnp.zeros((ZL, 128), F32)
     for k in range(8):
@@ -300,28 +316,32 @@
     ]
     for copy in qcopies:
         copy.start()
+    for copy in gcopies:
+        copy.wait_send()
     for dy, dc in ((0, 1), (1, 0), (1, 1)):
         w = quad_of(dy, dc)
         pltpu.make_async_copy(fin.at[w], fin.at[w], qr_sem.at[w]).wait()
     out[...] = jnp.concatenate([fin[w][:, 0:96] for w in range(4)], axis=1)
 
-    for copy in xcopies + exchanges + list(acopies.values()) + ccopies + gcopies + qcopies:
+    for copy in qcopies:
         copy.wait_send()
 
 
 def body(field, x_factor, y_factor, species_basis_matrix):
     vmem = pl.BlockSpec(memory_space=pltpu.VMEM)
     dma = pltpu.SemaphoreType.DMA
+    factors = (
+        jnp.pad(y_factor.T.astype(F32), ((0, XL + 8), (0, 0)))
+        + jnp.pad(x_factor.astype(F32), ((RJ, 8), (0, 128 - RI)))
+        + jnp.pad(species_basis_matrix.T, ((RJ + XL, 8 - RP), (0, 128 - NS)))
+    )
     return pl.pallas_call(
         kernel,
         out_shape=jax.ShapeDtypeStruct((ZL, NGZ * ZL), F32),
-        in_specs=[pl.BlockSpec(memory_space=pltpu.HBM)] * 4,
+        in_specs=[pl.BlockSpec(memory_space=pltpu.HBM), vmem],
         out_specs=vmem,
         scratch_shapes=[
             pltpu.VMEM((NS, XL, ZL, 128), BF16),
-            pltpu.VMEM((XL, RI), BF16),
-            pltpu.VMEM((RJ, 128), BF16),
-            pltpu.VMEM((RP, NS), F32),
             pltpu.VMEM((1024, 256), BF16),
             pltpu.VMEM((1024, 256), BF16),
             pltpu.VMEM((XL * ZL, 128), F32),
@@ -342,11 +362,11 @@
             pltpu.VMEM((256, 1152), BF16),
             pltpu.VMEM((8, ZL, 128), BF16),
             pltpu.VMEM((4, ZL, 128), F32),
-            dma((CH,)), dma((3,)), dma((CH,)), dma((CH,)), dma((NGX,)), dma((NGX,)), dma((NGX,)), dma((NGX,)),
+            dma((CH,)), dma((CH,)), dma((CH,)), dma((NGX,)), dma((NGX,)), dma((NGX,)), dma((NGX,)),
             dma((12,)), dma((12,)), dma((8,)), dma((8,)), dma((4,)), dma((4,)),
         ],
-        compiler_params=pltpu.CompilerParams(collective_id=0, has_side_effects=True, vmem_limit_bytes=56 * 1024 * 1024),
-    )(field, x_factor, y_factor.T, species_basis_matrix.T)
+        compiler_params=pltpu.CompilerParams(collective_id=0, has_side_effects=True, vmem_limit_bytes=53 * 1024 * 1024),
+    )(field, factors)
 
 
 def solution(mesh):

time: 41.9 us -> 39.3 us (0.938)
  Pallas kernels: 40.2 us -> 37.7 us
  local copies, waits for them, and re-layouts: 1.52 us -> 0.64 us
  other arithmetic: 0 us -> 0.74 us
    pallas_call x1, Pallas kernels: 40.2 us -> 37.7 us  [body(): pl.pallas_call(kernel, out_shape=jax.ShapeDtypeStruct((ZL, NGZ * ZL), F32...]
    unnamed x1, local copies, waits for them, and re-layouts: 1.52 us -> 0.64 us
    add x0 -> x1, other arithmetic: none -> 0.74 us  [body(): jnp.pad(y_factor.T.astype(F32), ((0, XL + 8), (0, 0)))]
where the time goes in v4:
time: 39.3 us; the launch traced here: 39.1 us
  Pallas kernels  37.7 us (96%)
  other arithmetic  0.74 us (2%)
  local copies, waits for them, and re-layouts  0.64 us (2%)
    pallas_call x1, Pallas kernels, body(): pl.pallas_call(kernel, out_shape=jax.ShapeDtypeStruct((ZL, NGZ * ZL), F32...  37.7 us

profile of v4, /device:TPU:1, one launch (start us, length us, event | category | flops | bytes accessed | tf_op | source)
XLA Modules:
  0.0 39.1 jit_solution(5550540431138990815)
XLA Ops:
  0.0 0.7 %pad_add_fusion.factors = f32[80,128]{1,0:T(8,128)S(1)} fusion(f32[4,8]{1,0:T(4,128)} %bitcast.3, bf16[24,48]{1,0:T(8,128)(2,1)} %param.5, bf16[48,128]{1,0:T(8,128)(2,1)} %bitcast.2), kind=kLoop, calls=%fused_computation | loop fusion | flops 40960 | bytes 55680 | tf_op jit(solution)/shard_map/add | solution.py:334
  0.7 37.7 %shard_map.46 = f32[48,384]{1,0:T(8,128)S(1)} custom-call(bf16[8,24,48,128]{3,2,1,0:T(8,128)(2,1)} %field.1, f32[80,128]{1,0:T(8,128)S(1)} %pad_add_fusion.factors), custom_call_target="tpu_custom_call" | custom-call | tf_op jit(solution)/shard_map/pallas_call | solution.py:338
  38.5 0.6 %copy.6 = f32[48,384]{1,0:T(8,128)} copy(f32[48,384]{1,0:T(8,128)S(1)} %shard_map.46) | data formatting | bytes 147456

commit v5 on v4

--- a/solution.py
+++ b/solution.py
@@ -21,8 +21,8 @@
 BIAS = 124.0
 SHARE = 6
 CH = 4
-ROWS = XL * ZL // CH
 FAR = (4, 12, 3, 11, 5, 13, 2, 10, 6, 14, 1, 9, 7, 15, 8)
+PLACES = FAR + (0,)
 
 
 def rem(number, by):
@@ -58,7 +58,7 @@
     return high, (value - high.astype(F32)).astype(BF16)
 
 
-def kernel(field, factors, out, fbuf, whi, wlo, mine, other, prt, tsum, xsend, xrecv, bd, asend, arecv,
+def kernel(field, factors, out, fbuf, whi, wlo, mine, away, packed, other, prt, xsend, xrecv, bd, asend, arecv,
            acc, d2, csend, owns, theirs, left_buf, right_buf, gsum, fin,
            f_sem, es_sem, er_sem, xs_sem, xr_sem, as_sem, ar_sem, cs_sem, cr_sem, gs_sem, gr_sem, qs_sem, qr_sem):
     gx, gz, gy = lax.axis_index("gx"), lax.axis_index("gz"), lax.axis_index("gy")
@@ -110,7 +110,11 @@
 
     lane = lax.broadcasted_iota(jnp.int32, (RJ, 256), 1)
     q = lane & 7
-    dest = (gx + ((lane >> 3) & 15)) & 15
+    place = (lane >> 3) & 15
+    dest = gx + jnp.zeros((RJ, 256), jnp.int32)
+    for n, dd in enumerate(PLACES):
+        dest = dest + jnp.where(place == n, dd, 0)
+    dest = dest & 15
     late = (q >= 3).astype(jnp.int32)
     jl = 3 * dest + q - 3 * late
     pick = (lax.broadcasted_iota(jnp.int32, (RJ, 256), 0) == jl) & (q < SHARE)
@@ -125,23 +129,51 @@
         whi[128 * s:128 * s + 128, :] = high
         wlo[128 * s:128 * s + 128, :] = rest
 
-    spare = lax.broadcasted_iota(jnp.int32, (ROWS, 128), 1) & 7
     for load in loads:
         load.wait()
     left = jnp.concatenate([fbuf[s].reshape(XL * ZL, 128) for s in range(NS)], axis=1)
     part = jnp.dot(left, whi[...], preferred_element_type=F32) + jnp.dot(left, wlo[...], preferred_element_type=F32)
     mine[...] = part[:, 0:128]
+    away[...] = part[:, 128:256]
+    largest = jnp.max(jnp.abs(part[:, 0:128]), keepdims=True)
+    unit = scale_of(jnp.max(jnp.abs(part[:, 128:256]), keepdims=True))
+    inverse = 1.0 / unit
+
+    line = lax.broadcasted_iota(jnp.int32, (NGX, 8, 128), 1)
+    scale_row = lax.broadcasted_iota(jnp.int32, (4, 64, 128), 1) == 48 + SHARE
+
+    def tile(rows, zg):
+        pieces = []
+        for zz in range(ZZ):
+            z = zg + ZG * zz
+            pieces.append(rows[pl.ds(z, XL, stride=ZL), :] if z < ZL else jnp.zeros((XL, 128), F32))
+        pieces.append(jnp.zeros((8, 128), F32))
+        return jnp.concatenate(pieces, axis=0).T.reshape(NGX, 8, 128)
+
+    def pairs(rows):
+        tails = (tile(rows, 8), tile(rows, 9))
+        for m in range(4):
+            both = []
+            for zg in (2 * m, 2 * m + 1):
+                one = tile(rows, zg)
+                both.append(jnp.where(line < SHARE, one, pltpu.roll(tails[zg // 3], 6 - 2 * (zg % 3), axis=1)) if zg < 6 else one)
+            yield pl.ds(16 * m, 16), both
+
+    for at, (a, b) in pairs(away):
+        a, b = encode(a, inverse), encode(b, inverse)
+        if at.start == 48:
+            a = jnp.where(line == SHARE, unit.reshape(1, 1, 1), a)
+        other[:, at, :] = jnp.concatenate([a, b], axis=1).astype(BF16)
+    for at, both in pairs(mine):
+        packed[:, at, :] = jnp.concatenate(both, axis=1)
+
     pl.semaphore_wait(barrier, NGX - 1 + 2 + NGZ - 1)
     exchanges = []
-    for c in range(CH):
-        span = pl.ds(c * ROWS, ROWS)
-        away = part[c * ROWS:c * ROWS + ROWS, 128:256]
-        unit = scale_of(jnp.max(jnp.abs(away), keepdims=True))
-        other[span, :] = jnp.where(spare == SHARE, unit, encode(away, 1.0 / unit)).astype(BF16)
+    for c in range(4):
+        group = pl.ds(4 * c, 4)
         exchanges.append(pltpu.make_async_remote_copy(
-            other.at[span], prt.at[span], es_sem.at[c], er_sem.at[c], device_id=in_quad(0, 1), device_id_type=MESH))
+            other.at[group], prt.at[group], es_sem.at[c], er_sem.at[c], device_id=in_quad(0, 1), device_id_type=MESH))
         exchanges[-1].start()
-
     xcopies = [
         pltpu.make_async_remote_copy(xsend, xrecv.at[dd], xs_sem.at[dd], xr_sem.at[dd], device_id=to_gx(dd), device_id_type=MESH)
         for dd in FAR
@@ -149,43 +181,23 @@
     for copy in xcopies:
         copy.start()
 
-    largest = jnp.zeros((8, 128), F32)
-    for c in range(CH):
+    acopies = {}
+    for c in range(4):
         exchanges[c].wait_recv()
-        span = pl.ds(c * ROWS, ROWS)
-        came = prt[span, :].astype(F32)
-        total = mine[span, :] + jnp.where(spare < SHARE, decode(came) * came[0:1, SHARE:SHARE + 1], 0.0)
-        tsum[span, :] = total
-        largest = jnp.maximum(largest, jnp.max(jnp.abs(total).reshape(ROWS // 8, 8, 128), axis=0))
-    unit = scale_of(jnp.max(largest, keepdims=True))
-    inverse = 1.0 / unit
-
-    line = lax.broadcasted_iota(jnp.int32, (NGX, 8, 128), 1)
-
-    def coded(zg):
-        pieces = []
-        for zz in range(ZZ):
-            z = zg + ZG * zz
-            pieces.append(tsum[pl.ds(z, XL, stride=ZL), :] if z < ZL else jnp.zeros((XL, 128), F32))
-        pieces.append(jnp.zeros((8, 128), F32))
-        return encode(jnp.concatenate(pieces, axis=0).T, inverse).reshape(NGX, 8, 128)
-
-    tails = (coded(8), coded(9))
-
-    def packed(zg):
-        if zg < 6:
-            return jnp.where(line < SHARE, coded(zg), pltpu.roll(tails[zg // 3], 6 - 2 * (zg % 3), axis=1))
-        return jnp.where(line == SHARE, unit.reshape(1, 1, 1), coded(zg))
-
-    for m in range(4):
-        asend[:, 16 * m:16 * m + 16, :] = jnp.concatenate([packed(2 * m), packed(2 * m + 1)], axis=1).astype(BF16)
-
-    acopies = {
-        dd: pltpu.make_async_remote_copy(asend.at[dd], arecv.at[dd], as_sem.at[dd], ar_sem.at[dd], device_id=to_gx(dd), device_id_type=MESH)
-        for dd in range(1, NGX)
-    }
-    for dd in FAR:
-        acopies[dd].start()
+        group = pl.ds(4 * c, 4)
+        came = prt[group].astype(F32)
+        if c == 0:
+            theirs_unit = came[0, 48 + SHARE:48 + SHARE + 1, 0:1]
+            unit = scale_of(largest + theirs_unit * TOP)
+            inverse = 1.0 / unit
+        total = packed[group] + decode(came) * theirs_unit.reshape(1, 1, 1)
+        asend[group] = jnp.where(scale_row, unit.reshape(1, 1, 1), encode(total, inverse)).astype(BF16)
+        for n in range(4 * c, 4 * c + 4):
+            dd = PLACES[n]
+            if dd:
+                acopies[dd] = pltpu.make_async_remote_copy(
+                    asend.at[n], arecv.at[n], as_sem.at[dd], ar_sem.at[dd], device_id=to_gx(dd), device_id_type=MESH)
+                acopies[dd].start()
 
     for copy in xcopies:
         copy.wait_recv()
@@ -202,18 +214,18 @@
     upper = jnp.dot(everything, first, preferred_element_type=F32)
     lower = jnp.dot(everything, second, preferred_element_type=F32)
     column = slot[0:XL]
-    for dd in range(NGX):
+    for n, dd in enumerate((0,) + FAR):
         block = jnp.concatenate([upper[16 * dd:16 * dd + 16], lower[16 * dd:16 * dd + 8]], axis=0)
         stack = [jnp.where(column == zz, block, 0.0) for zz in range(ZZ)] + [jnp.zeros((8, 256), F32)]
-        bd[128 * dd:128 * dd + 128, :] = jnp.concatenate(stack, axis=0).astype(BF16)
+        bd[128 * n:128 * n + 128, :] = jnp.concatenate(stack, axis=0).astype(BF16)
 
     eight = lax.broadcasted_iota(jnp.int32, (8, 128), 0)
     for k in range(NGX // 2):
         sides = []
-        for dd in (2 * k, 2 * k + 1):
+        for dd in ((0,) + FAR)[2 * k:2 * k + 2]:
             if dd:
                 acopies[dd].wait_recv()
-            held = (arecv if dd else asend)[dd].astype(F32)
+            held = (arecv if dd else asend)[PLACES.index(dd)].astype(F32)
             value = decode(held) * held[48 + SHARE:48 + SHARE + 1, :]
             tails = []
             for t in range(2):
@@ -345,9 +357,10 @@
             pltpu.VMEM((1024, 256), BF16),
             pltpu.VMEM((1024, 256), BF16),
             pltpu.VMEM((XL * ZL, 128), F32),
-            pltpu.VMEM((XL * ZL, 128), BF16),
-            pltpu.VMEM((XL * ZL, 128), BF16),
             pltpu.VMEM((XL * ZL, 128), F32),
+            pltpu.VMEM((NGX, 64, 128), F32),
+            pltpu.VMEM((NGX, 64, 128), BF16),
+            pltpu.VMEM((NGX, 64, 128), BF16),
             pltpu.VMEM((16, 128), BF16),
             pltpu.VMEM((NGX, 16, 128), BF16),
             pltpu.VMEM((NGX * 128, 256), BF16),

time: 39.3 us -> 38.6 us (0.982)
  Pallas kernels: 37.7 us -> 37.1 us
    pallas_call x1, Pallas kernels: 37.7 us -> 37.1 us  [body(): pl.pallas_call(kernel, out_shape=jax.ShapeDtypeStruct((ZL, NGZ * ZL), F32...]
where the time goes in v5:
time: 38.6 us; the launch traced here: 38.5 us
  Pallas kernels  37.1 us (96%)
  other arithmetic  0.74 us (2%)
  local copies, waits for them, and re-layouts  0.64 us (2%)
    pallas_call x1, Pallas kernels, body(): pl.pallas_call(kernel, out_shape=jax.ShapeDtypeStruct((ZL, NGZ * ZL), F32...  37.1 us

profile of v5, /device:TPU:1, one launch (start us, length us, event | category | flops | bytes accessed | tf_op | source)
XLA Modules:
  0.0 38.5 jit_solution(10863649552113183435)
XLA Ops:
  0.0 0.7 %pad_add_fusion.factors = f32[80,128]{1,0:T(8,128)S(1)} fusion(f32[4,8]{1,0:T(4,128)} %bitcast.3, bf16[24,48]{1,0:T(8,128)(2,1)} %param.5, bf16[48,128]{1,0:T(8,128)(2,1)} %bitcast.2), kind=kLoop, calls=%fused_computation | loop fusion | flops 40960 | bytes 55680 | tf_op jit(solution)/shard_map/add | solution.py:346
  0.7 37.1 %shard_map.46 = f32[48,384]{1,0:T(8,128)S(1)} custom-call(bf16[8,24,48,128]{3,2,1,0:T(8,128)(2,1)} %field.1, f32[80,128]{1,0:T(8,128)S(1)} %pad_add_fusion.factors), custom_call_target="tpu_custom_call" | custom-call | tf_op jit(solution)/shard_map/pallas_call | solution.py:350
  37.8 0.6 %copy.6 = f32[48,384]{1,0:T(8,128)} copy(f32[48,384]{1,0:T(8,128)S(1)} %shard_map.46) | data formatting | bytes 147456

commit v6 on v5

--- a/solution.py
+++ b/solution.py
@@ -133,8 +133,8 @@
         load.wait()
     left = jnp.concatenate([fbuf[s].reshape(XL * ZL, 128) for s in range(NS)], axis=1)
     part = jnp.dot(left, whi[...], preferred_element_type=F32) + jnp.dot(left, wlo[...], preferred_element_type=F32)
-    mine[...] = part[:, 0:128]
-    away[...] = part[:, 128:256]
+    mine[0:XL * ZL, :] = part[:, 0:128]
+    away[0:XL * ZL, :] = part[:, 128:256]
     largest = jnp.max(jnp.abs(part[:, 0:128]), keepdims=True)
     unit = scale_of(jnp.max(jnp.abs(part[:, 128:256]), keepdims=True))
     inverse = 1.0 / unit
@@ -356,8 +356,8 @@
             pltpu.VMEM((NS, XL, ZL, 128), BF16),
             pltpu.VMEM((1024, 256), BF16),
             pltpu.VMEM((1024, 256), BF16),
-            pltpu.VMEM((XL * ZL, 128), F32),
-            pltpu.VMEM((XL * ZL, 128), F32),
+            pltpu.VMEM((XL * ZL + ZL, 128), F32),
+            pltpu.VMEM((XL * ZL + ZL, 128), F32),
             pltpu.VMEM((NGX, 64, 128), F32),
             pltpu.VMEM((NGX, 64, 128), BF16),
             pltpu.VMEM((NGX, 64, 128), BF16),

time: 38.6 us -> 38.6 us (level)
  no operation moved by 1% of the time
where the time goes in v6:
time: 38.6 us; the launch traced here: 38.5 us
  Pallas kernels  37.1 us (96%)
  other arithmetic  0.74 us (2%)
  local copies, waits for them, and re-layouts  0.64 us (2%)
    pallas_call x1, Pallas kernels, body(): pl.pallas_call(kernel, out_shape=jax.ShapeDtypeStruct((ZL, NGZ * ZL), F32...  37.1 us

profile of v6, /device:TPU:1, one launch (start us, length us, event | category | flops | bytes accessed | tf_op | source)
XLA Modules:
  0.0 38.5 jit_solution(4850807353018266487)
XLA Ops:
  0.0 0.7 %pad_add_fusion.factors = f32[80,128]{1,0:T(8,128)S(1)} fusion(f32[4,8]{1,0:T(4,128)} %bitcast.3, bf16[24,48]{1,0:T(8,128)(2,1)} %param.5, bf16[48,128]{1,0:T(8,128)(2,1)} %bitcast.2), kind=kLoop, calls=%fused_computation | loop fusion | flops 40960 | bytes 55680 | tf_op jit(solution)/shard_map/add | solution.py:346
  0.7 37.1 %shard_map.46 = f32[48,384]{1,0:T(8,128)S(1)} custom-call(bf16[8,24,48,128]{3,2,1,0:T(8,128)(2,1)} %field.1, f32[80,128]{1,0:T(8,128)S(1)} %pad_add_fusion.factors), custom_call_target="tpu_custom_call" | custom-call | tf_op jit(solution)/shard_map/pallas_call | solution.py:350
  37.8 0.6 %copy.6 = f32[48,384]{1,0:T(8,128)} copy(f32[48,384]{1,0:T(8,128)S(1)} %shard_map.46) | data formatting | bytes 147456
